TPU v7x, 32 devices: a whole 2x2x4 slice. The times are simulated.
32 devices in a mesh: kv: 4 (over z), blk: 8 (over y, x, core).
Axes of the slice: x: 2, y: 2, z: 4, core: 2. Of those that a mesh axis runs over, the one named last changes fastest.
Arguments:
- embeds: bfloat16 [1, 64, 3072], P(None, None, 'blk'), may hold values from -40 to 40
- attn_norm: float32 [3072], P('blk'), may hold values from 0.25 to 1.75
- query_key_value_weight: bfloat16 [3072, 5120], P('blk', 'kv'), may hold values from -0.109375 to 0.109375
- w_out: bfloat16 [3072, 3072], P('kv', 'blk'), may hold values from -0.109375 to 0.109375
- mlp_norm: float32 [3072], P('blk'), may hold values from 0.25 to 1.75
- w_gate: bfloat16 [3072, 8192], P('blk', 'kv'), may hold values from -0.109375 to 0.109375
- w_up: bfloat16 [3072, 8192], P('blk', 'kv'), may hold values from -0.109375 to 0.109375
- w_down: bfloat16 [8192, 3072], P('kv', 'blk'), may hold values from -0.0625 to 0.0625
- prompt_key_slots: bfloat16 [256, 8, 128, 128], P('blk', 'kv'), may hold values from -210 to 210
- prompt_value_slots: bfloat16 [256, 8, 128, 128], P('blk', 'kv'), may hold values from -6 to 6
- generated_keys: bfloat16 [64, 8, 127, 128], P('blk', 'kv'), may hold values from -10 to 10
- generated_values: bfloat16 [64, 8, 127, 128], P('blk', 'kv'), may hold values from -6 to 6
- parents: int32 [1, 64], P(None, 'blk'), may hold values from 0 to 7
- prompt_length: int32 [8], replicated, may hold values from 1024 to 8192
- tenant_bounds: int32 [5], replicated, may hold values from 0 to 8, as said below
- slot_table: int32 [256], P('blk'), may hold values from 0 to 256, as said below
Outputs:
- hidden_out: float32 [1, 64, 3072], P(None, None, 'blk')
- keys_out: bfloat16 [64, 8, 128, 128], P('blk', 'kv')
- values_out: bfloat16 [64, 8, 128, 128], P('blk', 'kv')
Inputs may be any that keep to these rules, and one draw needn't show every extreme that they name: parents[s, b] is the beam, among the 8 beams of b's request, whose cache beam b continues at step s. tenant_bounds[0] = 0 and tenant_bounds[4] = 8, strictly rising. `slot_table`: with L_t the largest prompt_length of tenant t's requests, every block j below ceil(L_t / 128) of every tenant t stands in exactly one slot as t * 64 + j, no other block stands anywhere, and 256 marks an empty slot.
All inputs are finite; a program needn't handle non-finite values.
Results may differ from a plain program's by a relative error of at most 0.012.
The roundings to bfloat16 on the way count: a program that leaves them out, or rounds other values in their place, can miss the bound.
Values may be sent and summed in bfloat16 or wider, within the bound.
A program may use at most 64 MiB of HBM per device.

v0:
```python
import math

import jax
import jax.numpy as jnp
from jax import lax
from jax.sharding import PartitionSpec as P

MODEL_WIDTH = 3072
QUERY_HEADS = 24
KEY_VALUE_HEADS = 8
HEAD_WIDTH = 128
REQUEST_BEAMS = 8
TENANT_COUNT = 4
BLOCK_POSITIONS = 128
PROMPT_BLOCKS = 64
EARLIER_TOKENS = 127
DECODE_STEPS = 1


masked_score = -1e30


def merged(part, axis, combine):
    gathered = jax.tree.map(lambda a: lax.all_gather(a, axis), part)

    def take(source):
        return jax.tree.map(lambda a: lax.dynamic_index_in_dim(a, source, 0, False), gathered)

    return lax.fori_loop(
        1, lax.axis_size(axis), lambda source, state: combine(state, take(source)), take(0)
    )


def rotate(values, angles):
    half = values.shape[-1] // 2
    first = values[..., :half]
    second = values[..., half:]
    cosine = jnp.cos(angles)
    sine = jnp.sin(angles)
    return jnp.concatenate(
        [first * cosine - second * sine, second * cosine + first * sine], axis=-1
    )


def angles_for(positions, head_size):
    half = head_size // 2
    freq = jnp.exp(jnp.arange(half, dtype=jnp.float32) * (-math.log(500000.0) / half))
    return positions.astype(jnp.float32)[:, None] * freq[None, :]


def combine_parts(first, second):
    top_first, mass_first, sum_first = first
    top_second, mass_second, sum_second = second
    larger = jnp.maximum(top_first, top_second)
    factor_first = jnp.exp(top_first - larger)
    factor_second = jnp.exp(top_second - larger)
    return (
        larger,
        mass_first * factor_first + mass_second * factor_second,
        sum_first * factor_first[..., None] + sum_second * factor_second[..., None],
    )


def across_heads(partial_value):
    return lax.psum(partial_value, "kv")


def body(
    embeds,
    attn_norm,
    query_key_value_weight,
    w_out,
    mlp_norm,
    w_gate,
    w_up,
    w_down,
    prompt_key_slots,
    prompt_value_slots,
    generated_keys,
    generated_values,
    parents,
    prompt_length,
    tenant_bounds,
    slot_table,
):
    blocks = lax.axis_size("blk")
    my_index = lax.axis_index("blk")
    all_rows = embeds.shape[1]
    own_rows = all_rows // blocks
    heads_kv = prompt_key_slots.shape[1]
    slots_here = prompt_key_slots.shape[0]
    keys_here = slots_here * BLOCK_POSITIONS
    group_queries = QUERY_HEADS // KEY_VALUE_HEADS
    col_width = group_queries + 2
    score_scale = 1.0 / math.sqrt(HEAD_WIDTH)
    unit_count = w_gate.shape[1]
    beam_req = jnp.arange(all_rows, dtype=jnp.int32) // REQUEST_BEAMS
    tenant_beam = jnp.sum(
        (beam_req[:, None] >= tenant_bounds[None, 1:TENANT_COUNT]).astype(jnp.int32), axis=1
    )
    length_beam = jnp.repeat(prompt_length, REQUEST_BEAMS)
    slot_tenant = jnp.repeat(slot_table // PROMPT_BLOCKS, BLOCK_POSITIONS)
    slot_pos = jnp.repeat(slot_table % PROMPT_BLOCKS * BLOCK_POSITIONS, BLOCK_POSITIONS) + jnp.tile(
        jnp.arange(BLOCK_POSITIONS, dtype=jnp.int32), slots_here
    )
    visible = (tenant_beam[:, None] == slot_tenant[None, :]) & (
        slot_pos[None, :] < length_beam[:, None]
    )
    prompt_mask = visible[None, :, None, :]
    keys_flat = prompt_key_slots.transpose(1, 0, 2, 3).reshape(heads_kv, keys_here, HEAD_WIDTH)
    values_flat = prompt_value_slots.transpose(1, 0, 2, 3).reshape(heads_kv, keys_here, HEAD_WIDTH)
    local_beam = jnp.arange(own_rows, dtype=jnp.int32)
    base_rows = local_beam // REQUEST_BEAMS * REQUEST_BEAMS
    trailing_zeros = jnp.zeros((own_rows, heads_kv, DECODE_STEPS, HEAD_WIDTH), jnp.bfloat16)
    cached_key_rows = jnp.concatenate([generated_keys, trailing_zeros], axis=2)
    cached_value_rows = jnp.concatenate([generated_values, trailing_zeros], axis=2)
    gen_pos = jnp.arange(EARLIER_TOKENS + DECODE_STEPS, dtype=jnp.int32)
    w_both = jnp.concatenate([w_gate, w_up], axis=1)
    residual = embeds[0].astype(jnp.float32)
    squares = jnp.sum(residual * residual, axis=1)
    normed = (residual * attn_norm).astype(jnp.bfloat16)
    partial_value = jnp.dot(normed, query_key_value_weight, preferred_element_type=jnp.float32)
    total = lax.psum(squares, "blk")
    projected_rows = lax.psum(partial_value, "blk")
    inverse = lax.rsqrt(total / MODEL_WIDTH + 1e-05)
    projected_rows = (projected_rows * inverse[:, None]).reshape(
        all_rows, heads_kv, col_width, HEAD_WIDTH
    )
    angle_all = angles_for(length_beam + EARLIER_TOKENS + 0, HEAD_WIDTH)
    query_rows = rotate(projected_rows[:, :, :group_queries], angle_all[:, None, None, :]).astype(
        jnp.bfloat16
    )
    own_proj = lax.dynamic_slice_in_dim(projected_rows, my_index * own_rows, own_rows, 0)
    own_angle = lax.dynamic_slice_in_dim(angle_all, my_index * own_rows, own_rows, 0)
    new_key = rotate(own_proj[:, :, group_queries], own_angle[:, None, :]).astype(jnp.bfloat16)
    new_value = own_proj[:, :, group_queries + 1].astype(jnp.bfloat16)
    parent_rows = base_rows + parents[0]
    cached_key_rows = (
        jnp.take(cached_key_rows, parent_rows, axis=0).at[:, :, EARLIER_TOKENS].set(new_key)
    )
    cached_value_rows = (
        jnp.take(cached_value_rows, parent_rows, axis=0).at[:, :, EARLIER_TOKENS].set(new_value)
    )
    grouped = query_rows.transpose(1, 0, 2, 3).reshape(
        heads_kv, all_rows * group_queries, HEAD_WIDTH
    )
    scores = jnp.einsum("kqd,knd->kqn", grouped, keys_flat, preferred_element_type=jnp.float32)
    scores = scores.reshape(heads_kv, all_rows, group_queries, keys_here) * score_scale
    top_score = jnp.max(jnp.where(prompt_mask, scores, masked_score), axis=3)
    weights = jnp.where(prompt_mask, jnp.exp(scores - top_score[..., None]), 0.0)
    total_mass = jnp.sum(weights, axis=3)
    flat_weights = weights.reshape(heads_kv, all_rows * group_queries, keys_here).astype(
        jnp.bfloat16
    )
    summed = jnp.einsum(
        "kqn,knd->kqd", flat_weights, values_flat, preferred_element_type=jnp.float32
    )
    summed = summed.reshape(heads_kv, all_rows, group_queries, HEAD_WIDTH)
    all_top, all_mass, all_sum = merged((top_score, total_mass, summed), "blk", combine_parts)
    prompt_top = lax.dynamic_slice_in_dim(all_top, my_index * own_rows, own_rows, 1)
    prompt_mass = lax.dynamic_slice_in_dim(all_mass, my_index * own_rows, own_rows, 1)
    prompt_sum = lax.dynamic_slice_in_dim(all_sum, my_index * own_rows, own_rows, 1)
    own_queries = lax.dynamic_slice_in_dim(query_rows, my_index * own_rows, own_rows, 0)
    gen_scores = (
        jnp.einsum(
            "bkgd,bknd->kbgn", own_queries, cached_key_rows, preferred_element_type=jnp.float32
        )
        * score_scale
    )
    live = (gen_pos <= EARLIER_TOKENS)[None, None, None, :]
    gen_top = jnp.max(jnp.where(live, gen_scores, masked_score), axis=3)
    best = jnp.maximum(prompt_top, gen_top)
    gen_weights = jnp.where(live, jnp.exp(gen_scores - best[..., None]), 0.0)
    shift = jnp.exp(prompt_top - best)
    full_mass = prompt_mass * shift + jnp.sum(gen_weights, axis=3)
    gen_sum = jnp.einsum(
        "kbgn,bknd->kbgd",
        gen_weights.astype(jnp.bfloat16),
        cached_value_rows,
        preferred_element_type=jnp.float32,
    )
    attended_output = (prompt_sum * shift[..., None] + gen_sum) / full_mass[..., None]
    heads_out = (
        attended_output.transpose(1, 0, 2, 3)
        .reshape(own_rows, heads_kv * group_queries * HEAD_WIDTH)
        .astype(jnp.bfloat16)
    )
    head_part = jnp.dot(
        lax.all_gather(heads_out, "blk", axis=0, tiled=True),
        w_out,
        preferred_element_type=jnp.float32,
    )
    after_attn = residual + across_heads(head_part)
    total2 = lax.psum(jnp.sum(after_attn * after_attn, axis=1), "blk")
    inverse2 = lax.rsqrt(total2 / MODEL_WIDTH + 1e-05)
    normed2 = (after_attn * mlp_norm).astype(jnp.bfloat16)
    mixed = lax.psum_scatter(
        jnp.dot(normed2, w_both, preferred_element_type=jnp.float32),
        "blk",
        scatter_dimension=0,
        tiled=True,
    )
    own_inverse = lax.dynamic_slice_in_dim(inverse2, my_index * own_rows, own_rows, 0)
    gate = mixed[:, :unit_count] * own_inverse[:, None]
    upper = mixed[:, unit_count:] * own_inverse[:, None]
    hidden = (jax.nn.silu(gate) * upper).astype(jnp.bfloat16)
    ff_part = jnp.dot(
        lax.all_gather(hidden, "blk", axis=0, tiled=True),
        w_down,
        preferred_element_type=jnp.float32,
    )
    outputs = [after_attn + across_heads(ff_part)]
    return (jnp.stack(outputs), cached_key_rows, cached_value_rows)


def solution(mesh):
    in_specs = (
        P(None, None, "blk"),
        P("blk"),
        P("blk", "kv"),
        P("kv", "blk"),
        P("blk"),
        P("blk", "kv"),
        P("blk", "kv"),
        P("kv", "blk"),
        P("blk", "kv", None, None),
        P("blk", "kv", None, None),
        P("blk", "kv", None, None),
        P("blk", "kv", None, None),
        P(None, "blk"),
        P(),
        P(),
        P("blk"),
    )
    out_specs = (P(None, None, "blk"), P("blk", "kv", None, None), P("blk", "kv", None, None))
    return jax.shard_map(body, mesh=mesh, in_specs=in_specs, out_specs=out_specs, check_vma=False)
```

profile of v0, /device:TPU:0, one launch (start us, length us, event | category | flops | bytes accessed | tf_op | source)
XLA Modules:
  0.0 268.6 jit_solution(7508614428993247870)
XLA Ops:
  7.2 2.3 fusion.25
  9.6 0.9 fusion.21
  10.6 15.1 %psum.36 = f32[64]{0:T(128)S(1)} all-reduce(f32[64]{0:T(128)S(1)} %fusion.21), channel_id=1, replica_groups=mesh['kv'=4,'blk'=8] {'blk'}, use_global_device_ids=true, to_apply=%region_3.4 | all-reduce | flops 64 | bytes 512 | tf_op jit(solution)/shard_map/psum | solution.py:123
  25.7 0.7 broadcast_in_dim.88
  26.5 0.7 and_select_fusion.2
  27.2 0.7 slice.84
  28.1 0.3 compare_and_fusion
  28.4 1.2 broadcast_in_dim.89
  29.6 1.5 broadcast_in_dim.90
  31.1 3.3 %copy.139 = bf16[32,2,128,128]{3,2,0,1:T(8,128)(2,1)} copy(bf16[32,2,128,128]{3,2,1,0:T(8,128)(2,1)} %param.32) | data formatting | bytes 4194304 | tf_op args[8]
  34.4 1.5 copy.143
  35.9 0.8 broadcast_multiply_fusion.1
  36.7 31.7 %all-reduce.6.cloned.1.call-done = f32[64,1280]{1,0:T(8,128)} async-done(((f32[64,1280]{1,0:T(8,128)}), f32[64,1280]{1,0:T(8,128)}) %all-reduce.6.cloned.1.call-update) | async-done | bytes 327696 | tf_op jit(solution)/shard_map/psum | solution.py:124
  68.4 1.1 broadcast_multiply_fusion
  69.6 0.2 fusion.49
  69.9 0.2 maximum_bitcast_fusion
  70.3 3.4 %select_reduce_fusion = (f32[2,192]{1,0:T(2,128)S(1)}, f32[2,192,4096]{2,1,0:T(8,128)S(1)}) fusion(pred[192,4096]{1,0:T(8,128)(4,1)S(1)} %broadcast_in_dim.90, bf16[2,4096,128]{2,1,0:T(8,128)(2,1)} %bitcast.76, bf16[2,192,128]{2,0,1:T(2,128)(2,1)S(1)} %bitcast.79), kind=kOutput, calls=%fused_computation.13 | convolution fusion | flops 407371392 | bytes 9274880 | tf_op jit(solution)/shard_map/kqd,knd->kqn/dot_general | solution.py:147
  73.7 1.8 fusion.6
  75.5 0.9 copy-done.1
  76.5 0.7 copy.145
  77.3 1.1 copy.149
  78.4 1.1 copy.155
  79.7 0.8 concatenate.35
  80.5 1.4 gather_fusion
  81.9 2.5 gather_fusion.1
  84.4 0.5 iota_compare_fusion
  84.9 0.7 dynamic-slice_cosine_fusion
  85.7 2.2 broadcast_select_fusion.1
  87.8 0.8 all_gather.21
  88.6 4.4 %fusion.5 = f32[2,192]{1,0:T(2,128)S(1)} fusion(f32[2,192,4096]{2,1,0:T(8,128)} %copy-done.1, f32[2,192]{1,0:T(2,128)S(1)} %get-tuple-element.281, pred[192,4096]{1,0:T(8,128)(4,1)S(1)} %broadcast_in_dim.90), kind=kLoop, calls=%fused_computation.16 | loop fusion | flops 4718208 | bytes 7080960 | tf_op jit(solution)/shard_map/reduce_sum | solution.py:151
  93.2 0.9 copy.141
  94.5 1.5 scatter.9
  96.0 8.4 %all_gather.24 = f32[8,2,64,3]{2,1,3,0:T(2,128)S(1)} all-gather(f32[1,2,64,3]{2,1,3,0:T(2,128)S(1)} %copy.142), channel_id=1, replica_groups=mesh['kv'=4,'blk'=8] {'blk'}, dimensions={0}, use_global_device_ids=true | all-gather | bytes 13824 | tf_op jit(solution)/shard_map/all_gather | solution.py:24
  104.3 8.7 %all_gather.22 = f32[8,2,64,3]{2,1,3,0:T(2,128)S(1)} all-gather(f32[1,2,64,3]{2,1,3,0:T(2,128)S(1)} %copy.141), channel_id=1, replica_groups=mesh['kv'=4,'blk'=8] {'blk'}, dimensions={0}, use_global_device_ids=true | all-gather | bytes 13824 | tf_op jit(solution)/shard_map/all_gather | solution.py:24
  113.0 1.2 select_reduce_fusion.1
  114.2 1.0 slice_bitcast_fusion
  115.4 14.0 %while.21 = (s32[]{:T(128)}, f32[2,64,3]{1,0,2:T(2,128)S(1)}, f32[2,64,3]{1,0,2:T(2,128)S(1)}, f32[2,64,3,128]{3,2,1,0:T(4,128)S(1)}, f32[8,2,64,3]{2,1,3,0:T(2,...) while((s32[]{:T(128)}, f32[2,64,3]{1,0,2:T(2,128)S(1)}, ...), condition=%wide.region_7.8_spmd, body=%wide.region_6.7_spmd.sunk | while | flops 149765 | bytes 1004695 | solution.py:29
  115.7 0.9 constant_dynamic-slice_fusion.3
  116.6 0.8 fusion.62
  117.7 0.9 constant_dynamic-slice_fusion.3
  118.6 0.8 fusion.62
  119.7 0.9 constant_dynamic-slice_fusion.3
  120.6 0.8 fusion.62
  121.7 0.9 constant_dynamic-slice_fusion.3
  122.6 0.8 fusion.62
  123.7 0.9 constant_dynamic-slice_fusion.3
  124.6 0.8 fusion.62
  125.7 0.9 constant_dynamic-slice_fusion.3
  126.6 0.8 fusion.62
  127.7 0.9 constant_dynamic-slice_fusion.3
  128.6 0.8 fusion.62
  129.7 0.2 fusion.30
  129.9 1.4 fusion.17
  131.3 8.8 %all_gather.26 = bf16[64,768]{1,0:T(8,128)(2,1)S(1)} all-gather(bf16[8,768]{1,0:T(8,128)(2,1)S(1)} %bitcast.81), channel_id=1, replica_groups=mesh['kv'=4,'blk'=8] {'blk'}, dimensions={0}, use_global_device_ids=true | all-gather | bytes 110592 | tf_op jit(solution)/shard_map/all_gather | solution.py:189
  140.0 0.9 fusion.50
  141.0 34.4 %all-reduce.8.cloned.1.call-done = f32[64,384]{1,0:T(8,128)} async-done(((f32[64,384]{1,0:T(8,128)}), f32[64,384]{1,0:T(8,128)}) %all-reduce.8.cloned.1.call-update) | async-done | bytes 98320 | tf_op jit(solution)/shard_map/psum | solution.py:65
  175.4 3.6 %fusion.8 = f32[64,4096]{1,0:T(8,128)} fusion(bf16[384,2048]{1,0:T(8,128)(2,1)} %param.30, bf16[384,2048]{1,0:T(8,128)(2,1)} %param.29, f32[384]{0:T(512)S(1)} %copy-done.10, f32[64,384]{1,0:T(8,128)} %all-reduce.8.cloned.1.call-done, bf16[1,64,384]{2,1,0:T(8,128)(2,1)S(1)} %copy-done.6), kind=kOutput, calls=%fused_computation.18 | convolution fusion | flops 207716352 | bytes 4343296 | tf_op jit(solution)/shard_map/dot_general | solution.py:198
  179.2 11.8 %psum.38 = f32[64]{0:T(128)S(1)} all-reduce(f32[64]{0:T(128)S(1)} %multiply_reduce_fusion), channel_id=1, replica_groups=mesh['kv'=4,'blk'=8] {'blk'}, use_global_device_ids=true, to_apply=%region_13.15 | all-reduce | flops 64 | bytes 512 | tf_op jit(solution)/shard_map/psum | solution.py:194
  191.1 23.8 %reduce-scatter.2.cloned.1.call-done = f32[8,4096]{1,0:T(8,128)} async-done(((f32[64,4096]{1,0:T(8,128)}), f32[8,4096]{1,0:T(8,128)}) %reduce-scatter.2.cloned.1.call-update) | async-done | bytes 131088 | tf_op jit(solution)/shard_map/reduce_scatter | solution.py:197
  214.9 1.0 fusion.24
  215.9 9.2 %all_gather.27 = bf16[64,2048]{1,0:T(8,128)(2,1)S(1)} all-gather(bf16[8,2048]{1,0:T(8,128)(2,1)S(1)} %fusion.24), channel_id=1, replica_groups=mesh['kv'=4,'blk'=8] {'blk'}, dimensions={0}, use_global_device_ids=true | all-gather | bytes 294912 | tf_op jit(solution)/shard_map/all_gather | solution.py:208
  225.1 1.0 fusion.51
  226.1 34.4 %all-reduce.10.cloned.1.call-done = f32[64,384]{1,0:T(8,128)} async-done(((f32[64,384]{1,0:T(8,128)}), f32[64,384]{1,0:T(8,128)}) %all-reduce.10.cloned.1.call-update) | async-done | bytes 98320 | tf_op jit(solution)/shard_map/psum | solution.py:65
  260.6 1.5 add_bitcast_fusion
  (89 shorter events, 3.9 us)
Async XLA Ops:
  7.2 217.9 %copy-start = (bf16[2048,384]{1,0:T(8,128)(2,1)S(1)}, bf16[2048,384]{1,0:T(8,128)(2,1)}, u32[]{:S(2)}) copy-start(bf16[2048,384]{1,0:T(8,128)(2,1)} %param.31) | copy-start | bytes 4718596
  7.2 61.2 %all-reduce.6.cloned.1.call-start = ((), (), s32[]{:S(2)}) async-start(), calls=%async_computation.1 | async-start | bytes 655360 | tf_op jit(solution)/shard_map/psum | solution.py:124
  9.6 104.6 %all-gather.2.cloned.1.call-start = ((), (), s32[]{:S(2)}) async-start(), calls=%async_computation.2 | async-start | bytes 1769472 | tf_op jit(solution)/shard_map/all_gather | solution.py:24
  31.1 3.3 %copy-start.3 = (bf16[32,2,128,128]{3,2,1,0:T(8,128)(2,1)S(1)}, bf16[32,2,128,128]{3,2,1,0:T(8,128)(2,1)}, u32[]{:S(2)}) copy-start(bf16[32,2,128,128]{3,2,1,0:T(8,128)(2,1)} %param.33) | copy-start | bytes 6291460
  69.9 3.8 %copy-start.5 = (bf16[64,2,3,64]{3,2,0,1:T(4,128)(2,1)}, bf16[64,2,3,64]{3,2,0,1:T(4,128)(2,1)S(1)}, u32[]{:S(2)}) copy-start(bf16[64,2,3,64]{3,2,0,1:T(4,128)(2,1)S(1)} %get-tuple-element.267) | copy-start | bytes 147460
  70.3 3.5 %copy-start.4 = (bf16[32,2,128,128]{3,2,0,1:T(8,128)(2,1)S(1)}, bf16[32,2,128,128]{3,2,0,1:T(8,128)(2,1)}, u32[]{:S(2)}) copy-start(bf16[32,2,128,128]{3,2,0,1:T(8,128)(2,1)} %copy.143) | copy-start | bytes 6291460
  73.7 2.6 copy-start.1
  76.4 4.1 %copy-start.11 = (s32[1,8]{1,0:T(1,128)S(1)}, s32[1,8]{1,0:T(1,128)}, u32[]{:S(2)}) copy-start(s32[1,8]{1,0:T(1,128)} %param.36) | copy-start | bytes 100
  77.2 98.1 %all-reduce.8.cloned.1.call-start = ((), (), s32[]{:S(2)}) async-start(), calls=%async_computation.3 | async-start | bytes 196608 | tf_op jit(solution)/shard_map/psum | solution.py:65
  94.5 20.9 %copy-start.2 = (bf16[8,2,128,128]{3,2,1,0:T(8,128)(2,1)}, bf16[8,2,128,128]{3,2,1,0:T(8,128)(2,1)S(1)}, u32[]{:S(2)}) copy-start(bf16[8,2,128,128]{3,2,1,0:T(8,128)(2,1)S(1)} %scatter.6) | copy-start | bytes 1572868
  115.3 14.3 %copy-start.9 = (pred[128]{0:T(512)(128)(4,1)S(1)}, pred[128]{0:T(512)(128)(4,1)}, u32[]{:S(2)}) copy-start(pred[128]{0:T(512)(128)(4,1)} %iota_compare_fusion) | copy-start | bytes 388
  115.3 24.7 %copy-start.7 = (bf16[768,384]{1,0:T(8,128)(2,1)S(1)}, bf16[768,384]{1,0:T(8,128)(2,1)}, u32[]{:S(2)}) copy-start(bf16[768,384]{1,0:T(8,128)(2,1)} %param.27) | copy-start | bytes 1769476
  115.4 60.0 %copy-start.6 = (bf16[1,64,384]{2,1,0:T(8,128)(2,1)S(1)}, bf16[1,64,384]{2,1,0:T(8,128)(2,1)}, u32[]{:S(2)}) copy-start(bf16[1,64,384]{2,1,0:T(8,128)(2,1)} %param.24) | copy-start | bytes 147460
  115.4 60.0 %copy-start.10 = (f32[384]{0:T(512)S(1)}, f32[384]{0:T(512)}, u32[]{:S(2)}) copy-start(f32[384]{0:T(512)} %param.28) | copy-start | bytes 4612
  140.9 74.0 %reduce-scatter.2.cloned.1.call-start = ((), (), s32[]{:S(2)}) async-start(), calls=%async_computation.4 | async-start | bytes 1179648 | tf_op jit(solution)/shard_map/reduce_scatter | solution.py:197
  175.4 3.7 %copy-start.8 = (f32[64,384]{1,0:T(8,128)S(1)}, f32[64,384]{1,0:T(8,128)}, u32[]{:S(2)}) copy-start(f32[64,384]{1,0:T(8,128)} %all-reduce.8.cloned.1.call-done) | copy-start | bytes 294916
  179.0 81.5 %all-reduce.10.cloned.1.call-start = ((), (), s32[]{:S(2)}) async-start(), calls=%async_computation.5 | async-start | bytes 196608 | tf_op jit(solution)/shard_map/psum | solution.py:65
Sparse Core Ops, SparseCore 0:
  11.7 56.7 all-reduce.5
  77.4 25.1 all-gather.1
  141.0 34.2 all-reduce.7
  179.1 35.7 reduce-scatter.1
  226.2 34.2 all-reduce.9
where the time goes:
time: 270 us; the launch traced here: 269 us
  waiting for transfers between devices  124 us (46%)
  blocking collectives  62 us (23%)
  local copies, waits for them, and re-layouts  32 us (12%)
  other arithmetic  20 us (7%)
  matrix products  15.6 us (6%)
  between operations  14.1 us (5%)
    psum x2, waiting for transfers between devices, across_heads(): return lax.psum(partial_value, 'kv')  68.8 us
    psum x1, waiting for transfers between devices, body(): projected_rows = lax.psum(partial_value, 'blk')  31.7 us
    reduce_scatter x1, waiting for transfers between devices, body(): lax.psum_scatter(jnp.dot(normed2, w_both, preferred_element_type=jnp.floa...  23.8 us
    all_gather x2, blocking collectives, merged(): gathered = jax.tree.map(lambda a: lax.all_gather(a, axis), part)  17.1 us
    psum x1, blocking collectives, body(): total = lax.psum(squares, 'blk')  15.1 us
    psum x1, blocking collectives, body(): total2 = lax.psum(jnp.sum(after_attn * after_attn, axis=1), 'blk')  11.8 us
    all_gather x1, blocking collectives, body(): lax.all_gather(hidden, 'blk', axis=0, tiled=True)  9.22 us
    all_gather x1, blocking collectives, body(): lax.all_gather(heads_out, 'blk', axis=0, tiled=True)  8.77 us
  transfers between devices with their start and end apart: 5, of which 4 were waited for; matrix products, arithmetic and copies ran while one was open for 12% of the time, Pallas kernels for 0%

commit v1 on v0

v1 whole, which is shorter than its diff:
```python
import functools
import math

import jax
import jax.numpy as jnp
from jax import lax
from jax.experimental import pallas as pl
from jax.experimental.pallas import tpu as pltpu
from jax.sharding import PartitionSpec as P

MODEL_WIDTH = 3072
GROUP = 3
HEAD = 128
BEAMS = 8
TENANTS = 4
BLOCK = 128
PROMPT = 8192
EARLIER = 127
COLS = (GROUP + 2) * HEAD
MASKED = -1e30
FLOOR = -1e29
MESH = pl.DeviceIdType.MESH
F32 = jnp.float32
BF16 = jnp.bfloat16


def split3(column, shape):
    hi = column.astype(BF16).astype(F32)
    rest = column - hi
    mid = rest.astype(BF16).astype(F32)
    low = rest - mid
    lane = lax.broadcasted_iota(jnp.int32, shape, len(shape) - 1)
    return jnp.where(lane == 0, hi, jnp.where(lane == 1, mid, jnp.where(lane == 2, low, 0.0)))


def dot_t(a, b):
    return lax.dot_general(a, b, (((1,), (1,)), ((), ())), preferred_element_type=F32)


def kernel(
    n, z, hk, slots, width, units,
    parents, lengths, bounds, table,
    embeds, attn_norm, mlp_norm,
    wqkv_h, wout_h, wgate_h, wup_h, wdown_h, pk_h, pv_h, gk_h, gv_h,
    hidden_out, keys_out, values_out,
    wqkv, wout, wgate, wup, wdown, pk, pv, gk, gv, local_sem,
    qs, qr, qall, os_, orx, oall, ys, kr, gs, gr, hall, fs, fr,
    low_b, high_b, sbuf, tmp,
    s1, r1, s2, r2, s3, r3, s4, r4, s5, r5, s6, r6, s7, r7, s8, r8,
):
    b = lax.axis_index("blk")
    k = lax.axis_index("kv")
    rows = n * BEAMS
    own_q = hk * GROUP * BEAMS
    per_head = GROUP * BEAMS
    scale = 1.0 / math.sqrt(HEAD)

    loads = [
        pltpu.make_async_copy(src, dst, local_sem.at[i])
        for i, (src, dst) in enumerate(
            [(wqkv_h, wqkv), (gk_h, gk), (gv_h, gv), (pk_h, pk), (pv_h, pv),
             (wout_h, wout), (wgate_h, wgate), (wup_h, wup), (wdown_h, wdown)]
        )
    ]
    for load in loads:
        load.start()
    l_qkv, l_gk, l_gv, l_pk, l_pv, l_out, l_gate, l_up, l_down = loads

    barrier = pltpu.get_barrier_semaphore()

    @pl.loop(1, n)
    def _(d):
        pl.semaphore_signal(barrier, inc=1, device_id={"blk": lax.rem(b + d, n)}, device_id_type=MESH)

    @pl.loop(1, z)
    def _(d):
        pl.semaphore_signal(barrier, inc=1, device_id={"kv": lax.rem(k + d, z)}, device_id_type=MESH)

    def exchange(axis, me, size, src_of, dst, ssem, rsem):
        def copy(other, slot):
            return pltpu.make_async_remote_copy(
                src_ref=src_of(other), dst_ref=dst.at[slot], send_sem=ssem.at[other],
                recv_sem=rsem.at[slot], device_id={axis: other}, device_id_type=MESH,
            )

        def start():
            @pl.loop(1, size)
            def _(d):
                copy(lax.rem(me + d, size), me).start()

        def arrived():
            @pl.loop(1, size)
            def _(d):
                other = lax.rem(me + d, size)
                copy(other, other).wait_recv()

        def sent():
            @pl.loop(1, size)
            def _(d):
                other = lax.rem(me + d, size)
                copy(other, other).wait_send()

        return start, arrived, sent

    blk = functools.partial(exchange, "blk", b, n)
    kvx = functools.partial(exchange, "kv", k, z)
    x_qkv = blk(lambda t: qs.at[t], qr, s1, r1)
    x_q = blk(lambda t: qall.at[b], qall, s2, r2)
    x_o = blk(lambda t: os_.at[t], orx, s3, r3)
    x_heads = blk(lambda t: oall.at[b], oall, s4, r4)
    x_attn = kvx(lambda t: kr.at[k], kr, s5, r5)
    x_mix = blk(lambda t: gs.at[t], gr, s6, r6)
    x_hid = blk(lambda t: hall.at[b], hall, s7, r7)
    x_ff = kvx(lambda t: fr.at[k], fr, s8, r8)

    residual = embeds[0].astype(F32)
    squares = jnp.sum(residual * residual, axis=1, keepdims=True)
    normed = (residual * attn_norm[...]).astype(BF16)
    l_qkv.wait()
    part = jnp.dot(normed, wqkv[...], preferred_element_type=F32)
    qs[:, :, : hk * COLS] = part.reshape(n, BEAMS, hk * COLS)
    qs[:, :, hk * COLS :] = jnp.broadcast_to(squares, (rows, HEAD)).reshape(n, BEAMS, HEAD)
    pl.semaphore_wait(barrier, n - 1 + z - 1)
    x_qkv[0]()

    @pl.loop(0, n)
    def _(t):
        tenant = sum((t >= bounds[i]).astype(jnp.int32) for i in range(1, TENANTS))
        first = tenant * PROMPT
        low_b[t] = jnp.full((per_head, HEAD), first, jnp.int32)
        high_b[t] = jnp.full((per_head, HEAD), first + lengths[t], jnp.int32)

    lane = lax.broadcasted_iota(jnp.int32, (BEAMS, HEAD), 1)
    half = HEAD // 2
    index = jnp.where(lane < half, lane, lane - half).astype(F32)
    freq = jnp.exp(index * (-math.log(500000.0) / half))
    position = jnp.full((BEAMS, HEAD), lengths[b] + EARLIER, jnp.int32).astype(F32)
    angle = position * freq
    cosine = jnp.cos(angle)
    sine = jnp.where(lane < half, -jnp.sin(angle), jnp.sin(angle))

    def rotated(u):
        return u * cosine + pltpu.roll(u, half, 1) * sine

    qr[b] = qs[b]
    x_qkv[1]()
    total = qr[0]
    for t in range(1, n):
        total = total + qr[t]
    inverse = lax.rsqrt(total[:, hk * COLS :] / MODEL_WIDTH + 1e-05)

    def piece(h, j):
        start = h * COLS + j * HEAD
        return total[:, start : start + HEAD] * inverse

    own_query = jnp.concatenate(
        [rotated(piece(h, g)) for h in range(hk) for g in range(GROUP)], axis=0
    ).astype(BF16)
    qall[b] = own_query
    x_q[0]()

    l_gk.wait()
    l_gv.wait()
    row = lax.broadcasted_iota(jnp.int32, (BLOCK, HEAD), 0)
    new = [
        ([rotated(piece(h, GROUP)) for h in range(hk)], gk, keys_out),
        ([piece(h, GROUP + 1) for h in range(hk)], gv, values_out),
    ]
    for i in range(BEAMS):
        parent = parents[0, i]
        for j, (rows_new, src, dst) in enumerate(new):
            for h in range(hk):
                tmp[j, h, :EARLIER] = src[parent, h].astype(F32)
                dst[i, h] = jnp.where(row == EARLIER, rows_new[h][i : i + 1], tmp[j, h]).astype(BF16)

    own_f = own_query.astype(F32)
    gen = []
    for h in range(hk):
        query = own_f[h * per_head : (h + 1) * per_head].astype(BF16)
        keys = keys_out[:, h].reshape(BEAMS * BLOCK, HEAD)
        vals = values_out[:, h].reshape(BEAMS * BLOCK, HEAD)
        scores = dot_t(query, keys) * scale
        beam = lax.broadcasted_iota(jnp.int32, scores.shape, 0) % BEAMS
        owner = lax.broadcasted_iota(jnp.int32, scores.shape, 1) // BLOCK
        scores = jnp.where(beam == owner, scores, MASKED)
        top = jnp.max(scores, axis=1, keepdims=True)
        weights = jnp.exp(scores - top)
        mass = jnp.sum(weights, axis=1, keepdims=True)
        summed = jnp.dot(weights.astype(BF16), vals, preferred_element_type=F32)
        gen.append((summed, top, mass))
    gen_sum, gen_top, gen_mass = (jnp.concatenate(a, axis=0) for a in zip(*gen))

    x_q[1]()
    l_pk.wait()
    l_pv.wait()
    all_rows = n * per_head
    chunk = min(4, slots)
    queries = qall[...].astype(F32)
    inner = lax.broadcasted_iota(jnp.int32, (all_rows, BLOCK), 1)
    for h in range(hk):
        query = queries[:, h * per_head : (h + 1) * per_head].reshape(all_rows, HEAD).astype(BF16)

        def score(i, top, h=h, query=query):
            keys = pk[pl.ds(i * chunk, chunk), h].reshape(chunk * BLOCK, HEAD)
            scores = dot_t(query, keys) * scale
            low = low_b[...].reshape(all_rows, HEAD)
            high = high_b[...].reshape(all_rows, HEAD)
            for j in range(chunk):
                place = inner + table[i * chunk + j] * BLOCK
                seen = (place >= low) & (place < high)
                one = jnp.where(seen, scores[:, j * BLOCK : (j + 1) * BLOCK], MASKED)
                sbuf[i * chunk + j] = one
                top = jnp.maximum(top, one)
            return top

        top = lax.fori_loop(0, slots // chunk, score, jnp.full((all_rows, BLOCK), FLOOR, F32))
        top = jnp.max(top, axis=1, keepdims=True)

        def weigh(i, state, h=h, top=top):
            mass, summed = state
            parts = []
            for j in range(chunk):
                one = jnp.exp(sbuf[i * chunk + j] - top)
                mass = mass + one
                parts.append(one.astype(BF16))
            vals = pv[pl.ds(i * chunk, chunk), h].reshape(chunk * BLOCK, HEAD)
            summed = summed + jnp.dot(
                jnp.concatenate(parts, axis=1), vals, preferred_element_type=F32
            )
            return mass, summed

        zero = jnp.zeros((all_rows, HEAD), F32)
        mass, summed = lax.fori_loop(0, slots // chunk, weigh, (zero, zero))
        mass = jnp.sum(mass, axis=1, keepdims=True)
        some = mass > 0.0
        mean = summed / jnp.where(some, mass, 1.0)
        level = jnp.where(some, top + jnp.log(jnp.where(some, mass, 1.0)), FLOOR)
        both = jnp.concatenate([mean, split3(level, (all_rows, HEAD))], axis=1)
        sbuf2 = both.reshape(n, per_head, 2 * HEAD)
        if h == 0:
            held = [sbuf2]
        else:
            held.append(sbuf2)
    os_[...] = jnp.concatenate(held, axis=1).astype(BF16)
    orx[b] = os_[b]
    x_o[0]()
    x_o[1]()

    gen_level = gen_top + jnp.log(gen_mass)
    means = [gen_sum / gen_mass]
    levels = [gen_level]
    for t in range(n):
        got = orx[t].astype(F32)
        means.append(got[:, :HEAD])
        levels.append(got[:, HEAD : HEAD + 1] + got[:, HEAD + 1 : HEAD + 2] + got[:, HEAD + 2 : HEAD + 3])
    best = functools.reduce(jnp.maximum, levels)
    shares = [jnp.exp(level - best) for level in levels]
    whole = functools.reduce(jnp.add, shares)
    merged = functools.reduce(jnp.add, [m * s for m, s in zip(means, shares)]) / whole
    oall[b] = merged.astype(BF16)
    x_heads[0]()
    x_heads[1]()

    heads = oall[...].astype(F32)
    heads = jnp.concatenate(
        [heads[:, j * BEAMS : (j + 1) * BEAMS].reshape(rows, HEAD) for j in range(hk * GROUP)], axis=1
    ).astype(BF16)
    l_out.wait()
    kr[k] = jnp.dot(heads, wout[...], preferred_element_type=F32).astype(BF16)
    x_attn[0]()
    x_attn[1]()
    summed = kr[0].astype(F32)
    for t in range(1, z):
        summed = summed + kr[t].astype(F32)
    after = residual + summed

    squares = jnp.sum(after * after, axis=1, keepdims=True)
    normed2 = (after * mlp_norm[...]).astype(BF16)
    l_gate.wait()
    gate = jnp.dot(normed2, wgate[...], preferred_element_type=F32).reshape(n, BEAMS, units)
    l_up.wait()
    up = jnp.dot(normed2, wup[...], preferred_element_type=F32).reshape(n, BEAMS, units)
    gs[:, :, :units] = jnp.concatenate([gate, up], axis=1).astype(BF16)
    three = split3(squares, (rows, HEAD)).reshape(n, BEAMS, HEAD)
    gs[:, :, units:] = jnp.concatenate([three, three], axis=1).astype(BF16)
    gr[b] = gs[b]
    x_mix[0]()
    x_mix[1]()
    total = gr[0].astype(F32)
    for t in range(1, n):
        total = total + gr[t].astype(F32)
    three = total[:BEAMS, units:]
    squares = three[:, 0:1] + three[:, 1:2] + three[:, 2:3]
    inverse2 = lax.rsqrt(squares / MODEL_WIDTH + 1e-05)
    gate = total[:BEAMS, :units] * inverse2
    up = total[BEAMS:, :units] * inverse2
    hidden = gate / (1.0 + jnp.exp(-gate)) * up
    part_units = units // 2
    hall[b] = jnp.concatenate([hidden[:, :part_units], hidden[:, part_units:]], axis=0).astype(BF16)
    x_hid[0]()
    x_hid[1]()

    hidden = hall[...].astype(F32)
    hidden = jnp.concatenate(
        [hidden[:, :BEAMS].reshape(rows, part_units), hidden[:, BEAMS:].reshape(rows, part_units)], axis=1
    ).astype(BF16)
    l_down.wait()
    fr[k] = jnp.dot(hidden, wdown[...], preferred_element_type=F32).astype(BF16)
    x_ff[0]()
    x_ff[1]()
    summed = fr[0].astype(F32)
    for t in range(1, z):
        summed = summed + fr[t].astype(F32)
    hidden_out[0] = after + summed

    for x in (x_qkv, x_q, x_o, x_heads, x_attn, x_mix, x_hid, x_ff):
        x[2]()


def body(
    embeds, attn_norm, wqkv, w_out, mlp_norm, w_gate, w_up, w_down,
    pk, pv, gk, gv, parents, lengths, bounds, table,
):
    n = lax.axis_size("blk")
    z = lax.axis_size("kv")
    slots, hk = pk.shape[:2]
    rows, width = embeds.shape[1:]
    units = w_gate.shape[1]
    own_q = hk * GROUP * BEAMS
    smem = pl.BlockSpec(memory_space=pltpu.SMEM)
    vmem = pl.BlockSpec(memory_space=pltpu.VMEM)
    hbm = pl.BlockSpec(memory_space=pl.ANY)
    like = [pltpu.VMEM(a.shape, a.dtype) for a in (wqkv, w_out, w_gate, w_up, w_down, pk, pv, gk, gv)]
    cache = jax.ShapeDtypeStruct((BEAMS, hk, BLOCK, HEAD), BF16)
    wide = hk * COLS + HEAD
    sems = []
    for size in (n, n, n, n, z, n, n, z):
        sems += [pltpu.SemaphoreType.DMA((size,))] * 2
    return pl.pallas_call(
        functools.partial(kernel, n, z, hk, slots, width, units),
        out_shape=(jax.ShapeDtypeStruct((1, rows, width), F32), cache, cache),
        in_specs=[smem] * 4 + [vmem] * 3 + [hbm] * 9,
        out_specs=(vmem, vmem, vmem),
        scratch_shapes=like
        + [pltpu.SemaphoreType.DMA((9,))]
        + [
            pltpu.VMEM((n, BEAMS, wide), F32),
            pltpu.VMEM((n, BEAMS, wide), F32),
            pltpu.VMEM((n, own_q, HEAD), BF16),
            pltpu.VMEM((n, own_q, 2 * HEAD), BF16),
            pltpu.VMEM((n, own_q, 2 * HEAD), BF16),
            pltpu.VMEM((n, own_q, HEAD), BF16),
            pltpu.VMEM((8, 128), F32),
            pltpu.VMEM((z, rows, width), BF16),
            pltpu.VMEM((n, 2 * BEAMS, units + HEAD), BF16),
            pltpu.VMEM((n, 2 * BEAMS, units + HEAD), BF16),
            pltpu.VMEM((n, 2 * BEAMS, units // 2), BF16),
            pltpu.VMEM((8, 128), F32),
            pltpu.VMEM((z, rows, width), BF16),
            pltpu.VMEM((n, GROUP * BEAMS, HEAD), jnp.int32),
            pltpu.VMEM((n, GROUP * BEAMS, HEAD), jnp.int32),
            pltpu.VMEM((slots, n * GROUP * BEAMS, BLOCK), F32),
            pltpu.VMEM((2, hk, BLOCK, HEAD), F32),
        ]
        + sems,
        compiler_params=pltpu.CompilerParams(
            collective_id=0, has_side_effects=True, vmem_limit_bytes=56 * 2**20
        ),
        name="decode_step",
    )(
        parents, lengths, bounds, table,
        embeds, attn_norm.reshape(1, width), mlp_norm.reshape(1, width),
        wqkv, w_out, w_gate, w_up, w_down, pk, pv, gk, gv,
    )


def solution(mesh):
    in_specs = (
        P(None, None, "blk"), P("blk"), P("blk", "kv"), P("kv", "blk"), P("blk"),
        P("blk", "kv"), P("blk", "kv"), P("kv", "blk"),
        P("blk", "kv", None, None), P("blk", "kv", None, None),
        P("blk", "kv", None, None), P("blk", "kv", None, None),
        P(None, "blk"), P(), P(), P("blk"),
    )
    out_specs = (P(None, None, "blk"), P("blk", "kv", None, None), P("blk", "kv", None, None))
    return jax.shard_map(body, mesh=mesh, in_specs=in_specs, out_specs=out_specs, check_vma=False)
```

time: 270 us -> 70.4 us (0.26)
  waiting for transfers between devices: 124 us -> 0 us
  blocking collectives: 62 us -> 0 us
  Pallas kernels: 0 us -> 58.8 us
  local copies, waits for them, and re-layouts: 32 us -> 10.7 us
  other arithmetic: 20 us -> 0 us
  matrix products: 15.6 us -> 0 us
  between operations: 14.1 us -> 0.65 us
    psum x3 -> x0, waiting for transfers between devices: 101 us -> none  [the longest x2 68.8 us: across_heads(): return lax.psum(partial_value, 'kv')]
    pallas_call x0 -> x1, Pallas kernels: none -> 58.8 us  [body(): pl.pallas_call(functools.partial(kernel, n, z, hk, slots, width, units),...]
    all_gather x4 -> x0, blocking collectives: 35 us -> none  [the longest x2 17.1 us: merged(): gathered = jax.tree.map(lambda a: lax.all_gather(a, axis), part)]
    psum x2 -> x0, blocking collectives: 26.9 us -> none  [the longest x1 15.1 us: body(): total = lax.psum(squares, 'blk')]
    reduce_scatter x1 -> x0, waiting for transfers between devices: 23.8 us -> none  [body(): lax.psum_scatter(jnp.dot(normed2, w_both, preferred_element_type=jnp.floa...]
    dot_general x8 -> x0, matrix products: 15.6 us -> none  [the longest x1 3.62 us: body(): jnp.dot(normed2, w_both, preferred_element_type=jnp.float32)]
    dynamic_slice x8 -> x0, local copies, waits for them, and re-layouts: 6.7 us -> none  [the longest x7 6.63 us: take(): lax.dynamic_index_in_dim(a, source, 0, False)]
    add x16 -> x0, other arithmetic: 5.82 us -> none  [the longest x7 5.53 us: combine_parts(): sum_first * factor_first[..., None] + sum_second * factor_second[..., None]]
  transfers between devices with their start and end apart: 5 -> 0, of which waited for: 4 -> 0; matrix products, arithmetic and copies ran while one was open for 12% -> 0% of each run, Pallas kernels for 0% -> 0%
where the time goes in v1:
time: 70.4 us; the launch traced here: 70.1 us
  Pallas kernels  58.8 us (84%)
  local copies, waits for them, and re-layouts  10.7 us (15%)
    pallas_call x1, Pallas kernels, body(): pl.pallas_call(functools.partial(kernel, n, z, hk, slots, width, units),...  58.8 us
    unnamed x7, local copies, waits for them, and re-layouts  8.15 us

profile of v1, /device:TPU:0, one launch (start us, length us, event | category | flops | bytes accessed | tf_op | source)
XLA Modules:
  0.0 70.1 jit_solution(4494419750894154163)
XLA Ops:
  0.6 1.2 %reshape.12.attn_norm = f32[1,384]{1,0:T(1,128)} reshape(f32[384]{0:T(512)} %param.17) | data formatting | bytes 3072 | tf_op jit(solution)/shard_map/reshape | solution.py:372
  1.9 1.3 %reshape.13.mlp_norm = f32[1,384]{1,0:T(1,128)} reshape(f32[384]{0:T(512)} %param.20) | data formatting | bytes 3072 | tf_op jit(solution)/shard_map/reshape | solution.py:372
  3.1 1.9 %copy.19.gk_h = bf16[8,2,127,128]{3,2,1,0:T(8,128)(2,1)} copy(bf16[8,2,127,128]{3,1,2,0:T(2,128)(2,1)} %param.26) | data formatting | bytes 1040384 | tf_op args[10]
  5.1 1.9 %copy.20.gv_h = bf16[8,2,127,128]{3,2,1,0:T(8,128)(2,1)} copy(bf16[8,2,127,128]{3,1,2,0:T(2,128)(2,1)} %param.27) | data formatting | bytes 1040384 | tf_op args[11]
  7.0 58.8 %decode_step.1 = (f32[1,64,384]{2,1,0:T(8,128)}, bf16[8,2,128,128]{3,2,1,0:T(8,128)(2,1)}, bf16[8,2,128,128]{3,2,1,0:T(8,128)(2,1)}) custom-call(s32[1,8]{1,0:T(1,128)} %parents.1, s32[8]{0:T(128)} %lengths.1, s32[5]{0:T(128)} %bounds.1, s32[32]{0:T(128)} %table.1, bf16[1,64,384]{2,1,0:T(8,128)(2,1)} %embeds.1, f32[1,384]{1,0:T(1,128)} %reshape.12.attn_norm, ...), custom_call_target="tpu_custom_call" | custom-call | tf_op jit(solution)/shard_map/decode_step/pallas_call | solution.py:339
  65.8 0.0 copy-start
  65.8 1.6 %copy.24 = f32[1,64,384]{2,1,0:T(8,128)} copy(f32[1,64,384]{2,1,0:T(8,128)} %get-tuple-element.6) | data formatting | bytes 196608
  67.4 1.9 %copy.25 = bf16[8,2,128,128]{3,2,1,0:T(8,128)(2,1)} copy(bf16[8,2,128,128]{3,2,1,0:T(8,128)(2,1)} %get-tuple-element.7) | data formatting | bytes 1048576
  69.3 0.0 copy-done
  69.3 0.8 %copy.26 = bf16[8,2,128,128]{3,2,1,0:T(8,128)(2,1)} copy(bf16[8,2,128,128]{3,2,1,0:T(8,128)(2,1)S(1)} %copy-done) | data formatting | bytes 1048576
Async XLA Ops:
  65.8 3.5 %copy-start = (bf16[8,2,128,128]{3,2,1,0:T(8,128)(2,1)S(1)}, bf16[8,2,128,128]{3,2,1,0:T(8,128)(2,1)}, u32[]{:S(2)}) copy-start(bf16[8,2,128,128]{3,2,1,0:T(8,128)(2,1)} %get-tuple-element.8) | copy-start | bytes 1572868

commit v2 on v1

--- a/solution.py
+++ b/solution.py
@@ -19,6 +19,7 @@
 COLS = (GROUP + 2) * HEAD
 MASKED = -1e30
 FLOOR = -1e29
+LOG2E = math.log2(math.e)
 MESH = pl.DeviceIdType.MESH
 F32 = jnp.float32
 BF16 = jnp.bfloat16
@@ -44,9 +45,9 @@
     wqkv_h, wout_h, wgate_h, wup_h, wdown_h, pk_h, pv_h, gk_h, gv_h,
     hidden_out, keys_out, values_out,
     wqkv, wout, wgate, wup, wdown, pk, pv, gk, gv, local_sem,
-    qs, qr, qall, os_, orx, oall, ys, kr, gs, gr, hall, fs, fr,
-    low_b, high_b, sbuf, tmp,
-    s1, r1, s2, r2, s3, r3, s4, r4, s5, r5, s6, r6, s7, r7, s8, r8,
+    qs, qr, qall, os_, orx, oall, ks, kr, ka, gs, gr, hall, fs, fr, fa,
+    bias, sbuf, gkf, gvf,
+    s1, r1, s2, r2, s3, r3, s4, r4, s5, r5, s6, r6, s7, r7, s8, r8, s9, r9, s10, r10,
 ):
     b = lax.axis_index("blk")
     k = lax.axis_index("kv")
@@ -62,7 +63,7 @@
              (wout_h, wout), (wgate_h, wgate), (wup_h, wup), (wdown_h, wdown)]
         )
     ]
-    for load in loads:
+    for load in loads[:3]:
         load.start()
     l_qkv, l_gk, l_gv, l_pk, l_pv, l_out, l_gate, l_up, l_down = loads
 
@@ -83,22 +84,21 @@
                 recv_sem=rsem.at[slot], device_id={axis: other}, device_id_type=MESH,
             )
 
+        def each(act):
+            if size <= 8:
+                for d in range(1, size):
+                    act(lax.rem(me + d, size))
+            else:
+                pl.loop(1, size)(lambda d: act(lax.rem(me + d, size)))
+
         def start():
-            @pl.loop(1, size)
-            def _(d):
-                copy(lax.rem(me + d, size), me).start()
+            each(lambda other: copy(other, me).start())
 
         def arrived():
-            @pl.loop(1, size)
-            def _(d):
-                other = lax.rem(me + d, size)
-                copy(other, other).wait_recv()
+            each(lambda other: copy(other, other).wait_recv())
 
         def sent():
-            @pl.loop(1, size)
-            def _(d):
-                other = lax.rem(me + d, size)
-                copy(other, other).wait_send()
+            each(lambda other: copy(other, other).wait_send())
 
         return start, arrived, sent
 
@@ -108,14 +108,29 @@
     x_q = blk(lambda t: qall.at[b], qall, s2, r2)
     x_o = blk(lambda t: os_.at[t], orx, s3, r3)
     x_heads = blk(lambda t: oall.at[b], oall, s4, r4)
-    x_attn = kvx(lambda t: kr.at[k], kr, s5, r5)
+    x_attn = kvx(lambda t: ks.at[t], kr, s5, r5)
+    x_attn2 = kvx(lambda t: ka.at[k], ka, s9, r9)
     x_mix = blk(lambda t: gs.at[t], gr, s6, r6)
     x_hid = blk(lambda t: hall.at[b], hall, s7, r7)
-    x_ff = kvx(lambda t: fr.at[k], fr, s8, r8)
+    x_ff = kvx(lambda t: fs.at[t], fr, s8, r8)
+    x_ff2 = kvx(lambda t: fa.at[k], fa, s10, r10)
+
+    def over_kv(part, send, got, every, scatter, gather):
+        send[...] = part.reshape(send.shape).astype(BF16)
+        got[k] = send[k]
+        scatter[0]()
+        scatter[1]()
+        summed = got[0].astype(F32)
+        for t in range(1, z):
+            summed = summed + got[t].astype(F32)
+        every[k] = summed.astype(BF16)
+        gather[0]()
+        gather[1]()
+        return every[...].astype(F32).reshape(rows, width)
 
     residual = embeds[0].astype(F32)
     squares = jnp.sum(residual * residual, axis=1, keepdims=True)
-    normed = (residual * attn_norm[...]).astype(BF16)
+    normed = (residual * attn_norm[...].reshape(1, width)).astype(BF16)
     l_qkv.wait()
     part = jnp.dot(normed, wqkv[...], preferred_element_type=F32)
     qs[:, :, : hk * COLS] = part.reshape(n, BEAMS, hk * COLS)
@@ -123,14 +138,25 @@
     pl.semaphore_wait(barrier, n - 1 + z - 1)
     x_qkv[0]()
 
+    for load in loads[3:]:
+        load.start()
+    lane = lax.broadcasted_iota(jnp.int32, (BEAMS, HEAD), 1)
+
     @pl.loop(0, n)
     def _(t):
         tenant = sum((t >= bounds[i]).astype(jnp.int32) for i in range(1, TENANTS))
-        first = tenant * PROMPT
-        low_b[t] = jnp.full((per_head, HEAD), first, jnp.int32)
-        high_b[t] = jnp.full((per_head, HEAD), first + lengths[t], jnp.int32)
-
-    lane = lax.broadcasted_iota(jnp.int32, (BEAMS, HEAD), 1)
+        last = lengths[t]
+
+        @pl.loop(0, slots)
+        def _(i):
+            place = table[i] * BLOCK - tenant * PROMPT + lane
+            bias[i, t] = jnp.where((place >= 0) & (place < last), 0.0, MASKED)
+
+    for load, src, dst in ((l_gk, gk, gkf), (l_gv, gv, gvf)):
+        load.wait()
+        dst[: src.shape[0]] = src[...].astype(F32)
+        dst[src.shape[0] :] = jnp.zeros((8, HEAD), F32)
+
     half = HEAD // 2
     index = jnp.where(lane < half, lane, lane - half).astype(F32)
     freq = jnp.exp(index * (-math.log(500000.0) / half))
@@ -159,19 +185,18 @@
     qall[b] = own_query
     x_q[0]()
 
-    l_gk.wait()
-    l_gv.wait()
     row = lax.broadcasted_iota(jnp.int32, (BLOCK, HEAD), 0)
     new = [
-        ([rotated(piece(h, GROUP)) for h in range(hk)], gk, keys_out),
-        ([piece(h, GROUP + 1) for h in range(hk)], gv, values_out),
+        ([rotated(piece(h, GROUP)) for h in range(hk)], gkf, keys_out),
+        ([piece(h, GROUP + 1) for h in range(hk)], gvf, values_out),
     ]
     for i in range(BEAMS):
         parent = parents[0, i]
-        for j, (rows_new, src, dst) in enumerate(new):
+        for rows_new, src, dst in new:
             for h in range(hk):
-                tmp[j, h, :EARLIER] = src[parent, h].astype(F32)
-                dst[i, h] = jnp.where(row == EARLIER, rows_new[h][i : i + 1], tmp[j, h]).astype(BF16)
+                first = parent * (EARLIER * hk) + h
+                old = src[pl.ds(first, BLOCK, stride=hk) if hk > 1 else pl.ds(first, BLOCK), :]
+                dst[i, h] = jnp.where(row == EARLIER, rows_new[h][i : i + 1], old).astype(BF16)
 
     own_f = own_query.astype(F32)
     gen = []
@@ -194,53 +219,49 @@
     l_pk.wait()
     l_pv.wait()
     all_rows = n * per_head
-    chunk = min(4, slots)
+    chunk = min(8, slots)
     queries = qall[...].astype(F32)
-    inner = lax.broadcasted_iota(jnp.int32, (all_rows, BLOCK), 1)
-    for h in range(hk):
-        query = queries[:, h * per_head : (h + 1) * per_head].reshape(all_rows, HEAD).astype(BF16)
-
-        def score(i, top, h=h, query=query):
-            keys = pk[pl.ds(i * chunk, chunk), h].reshape(chunk * BLOCK, HEAD)
-            scores = dot_t(query, keys) * scale
-            low = low_b[...].reshape(all_rows, HEAD)
-            high = high_b[...].reshape(all_rows, HEAD)
-            for j in range(chunk):
-                place = inner + table[i * chunk + j] * BLOCK
-                seen = (place >= low) & (place < high)
-                one = jnp.where(seen, scores[:, j * BLOCK : (j + 1) * BLOCK], MASKED)
-                sbuf[i * chunk + j] = one
-                top = jnp.maximum(top, one)
-            return top
-
-        top = lax.fori_loop(0, slots // chunk, score, jnp.full((all_rows, BLOCK), FLOOR, F32))
-        top = jnp.max(top, axis=1, keepdims=True)
-
-        def weigh(i, state, h=h, top=top):
-            mass, summed = state
-            parts = []
-            for j in range(chunk):
-                one = jnp.exp(sbuf[i * chunk + j] - top)
-                mass = mass + one
-                parts.append(one.astype(BF16))
-            vals = pv[pl.ds(i * chunk, chunk), h].reshape(chunk * BLOCK, HEAD)
-            summed = summed + jnp.dot(
-                jnp.concatenate(parts, axis=1), vals, preferred_element_type=F32
-            )
-            return mass, summed
-
-        zero = jnp.zeros((all_rows, HEAD), F32)
-        mass, summed = lax.fori_loop(0, slots // chunk, weigh, (zero, zero))
-        mass = jnp.sum(mass, axis=1, keepdims=True)
-        some = mass > 0.0
-        mean = summed / jnp.where(some, mass, 1.0)
-        level = jnp.where(some, top + jnp.log(jnp.where(some, mass, 1.0)), FLOOR)
-        both = jnp.concatenate([mean, split3(level, (all_rows, HEAD))], axis=1)
-        sbuf2 = both.reshape(n, per_head, 2 * HEAD)
-        if h == 0:
-            held = [sbuf2]
-        else:
-            held.append(sbuf2)
+    heads_q = [
+        queries[:, h * per_head : (h + 1) * per_head].reshape(all_rows, HEAD).astype(BF16)
+        for h in range(hk)
+    ]
+    zero = jnp.zeros((all_rows, HEAD), F32)
+    held = []
+    top = None
+    for step in range(hk + 1):
+
+        def both_passes(i, state, step=step, top=top):
+            high, mass, summed = state
+            if step < hk:
+                keys = pk[pl.ds(i * chunk, chunk), step].reshape(chunk * BLOCK, HEAD)
+                scores = dot_t(heads_q[step], keys)
+                for j in range(chunk):
+                    one = scores[:, j * BLOCK : (j + 1) * BLOCK].reshape(n, GROUP, BEAMS, BLOCK)
+                    one = (one + bias[i * chunk + j][:, None]).reshape(all_rows, BLOCK)
+                    sbuf[step % 2, i * chunk + j] = one
+                    high = jnp.maximum(high, one)
+            if step > 0:
+                parts = []
+                for j in range(chunk):
+                    one = jnp.exp2((sbuf[(step - 1) % 2, i * chunk + j] - top) * (scale * LOG2E))
+                    mass = mass + one
+                    parts.append(one.astype(BF16))
+                vals = pv[pl.ds(i * chunk, chunk), step - 1].reshape(chunk * BLOCK, HEAD)
+                summed = summed + jnp.dot(
+                    jnp.concatenate(parts, axis=1), vals, preferred_element_type=F32
+                )
+            return high, mass, summed
+
+        floor = jnp.full((all_rows, BLOCK), FLOOR, F32)
+        high, mass, summed = lax.fori_loop(0, slots // chunk, both_passes, (floor, zero, zero))
+        if step > 0:
+            mass = jnp.sum(mass, axis=1, keepdims=True)
+            some = mass > 0.0
+            safe = jnp.where(some, mass, 1.0)
+            level = jnp.where(some, top * scale + jnp.log(safe), FLOOR)
+            both = jnp.concatenate([summed / safe, split3(level, (all_rows, HEAD))], axis=1)
+            held.append(both.reshape(n, per_head, 2 * HEAD))
+        top = jnp.max(high, axis=1, keepdims=True)
     os_[...] = jnp.concatenate(held, axis=1).astype(BF16)
     orx[b] = os_[b]
     x_o[0]()
@@ -266,16 +287,12 @@
         [heads[:, j * BEAMS : (j + 1) * BEAMS].reshape(rows, HEAD) for j in range(hk * GROUP)], axis=1
     ).astype(BF16)
     l_out.wait()
-    kr[k] = jnp.dot(heads, wout[...], preferred_element_type=F32).astype(BF16)
-    x_attn[0]()
-    x_attn[1]()
-    summed = kr[0].astype(F32)
-    for t in range(1, z):
-        summed = summed + kr[t].astype(F32)
-    after = residual + summed
+    after = residual + over_kv(
+        jnp.dot(heads, wout[...], preferred_element_type=F32), ks, kr, ka, x_attn, x_attn2
+    )
 
     squares = jnp.sum(after * after, axis=1, keepdims=True)
-    normed2 = (after * mlp_norm[...]).astype(BF16)
+    normed2 = (after * mlp_norm[...].reshape(1, width)).astype(BF16)
     l_gate.wait()
     gate = jnp.dot(normed2, wgate[...], preferred_element_type=F32).reshape(n, BEAMS, units)
     l_up.wait()
@@ -305,16 +322,21 @@
         [hidden[:, :BEAMS].reshape(rows, part_units), hidden[:, BEAMS:].reshape(rows, part_units)], axis=1
     ).astype(BF16)
     l_down.wait()
-    fr[k] = jnp.dot(hidden, wdown[...], preferred_element_type=F32).astype(BF16)
-    x_ff[0]()
-    x_ff[1]()
-    summed = fr[0].astype(F32)
-    for t in range(1, z):
-        summed = summed + fr[t].astype(F32)
-    hidden_out[0] = after + summed
-
-    for x in (x_qkv, x_q, x_o, x_heads, x_attn, x_mix, x_hid, x_ff):
+    hidden_out[0] = after + over_kv(
+        jnp.dot(hidden, wdown[...], preferred_element_type=F32), fs, fr, fa, x_ff, x_ff2
+    )
+
+    for x in (x_qkv, x_q, x_o, x_heads, x_attn, x_attn2, x_mix, x_hid, x_ff, x_ff2):
         x[2]()
+
+
+def store(*refs):
+    sem = refs[6]
+    copies = [pltpu.make_async_copy(refs[i], refs[3 + i], sem.at[i]) for i in range(3)]
+    for copy in copies:
+        copy.start()
+    for copy in copies:
+        copy.wait()
 
 
 def body(
@@ -330,13 +352,14 @@
     smem = pl.BlockSpec(memory_space=pltpu.SMEM)
     vmem = pl.BlockSpec(memory_space=pltpu.VMEM)
     hbm = pl.BlockSpec(memory_space=pl.ANY)
+    gk, gv = (a.transpose(0, 2, 1, 3).reshape(-1, HEAD) for a in (gk, gv))
     like = [pltpu.VMEM(a.shape, a.dtype) for a in (wqkv, w_out, w_gate, w_up, w_down, pk, pv, gk, gv)]
     cache = jax.ShapeDtypeStruct((BEAMS, hk, BLOCK, HEAD), BF16)
     wide = hk * COLS + HEAD
     sems = []
-    for size in (n, n, n, n, z, n, n, z):
+    for size in (n, n, n, n, z, n, n, z, z, z):
         sems += [pltpu.SemaphoreType.DMA((size,))] * 2
-    return pl.pallas_call(
+    results = pl.pallas_call(
         functools.partial(kernel, n, z, hk, slots, width, units),
         out_shape=(jax.ShapeDtypeStruct((1, rows, width), F32), cache, cache),
         in_specs=[smem] * 4 + [vmem] * 3 + [hbm] * 9,
@@ -350,17 +373,19 @@
             pltpu.VMEM((n, own_q, 2 * HEAD), BF16),
             pltpu.VMEM((n, own_q, 2 * HEAD), BF16),
             pltpu.VMEM((n, own_q, HEAD), BF16),
-            pltpu.VMEM((8, 128), F32),
-            pltpu.VMEM((z, rows, width), BF16),
+            pltpu.VMEM((z, rows // z, width), BF16),
+            pltpu.VMEM((z, rows // z, width), BF16),
+            pltpu.VMEM((z, rows // z, width), BF16),
             pltpu.VMEM((n, 2 * BEAMS, units + HEAD), BF16),
             pltpu.VMEM((n, 2 * BEAMS, units + HEAD), BF16),
             pltpu.VMEM((n, 2 * BEAMS, units // 2), BF16),
-            pltpu.VMEM((8, 128), F32),
-            pltpu.VMEM((z, rows, width), BF16),
-            pltpu.VMEM((n, GROUP * BEAMS, HEAD), jnp.int32),
-            pltpu.VMEM((n, GROUP * BEAMS, HEAD), jnp.int32),
-            pltpu.VMEM((slots, n * GROUP * BEAMS, BLOCK), F32),
-            pltpu.VMEM((2, hk, BLOCK, HEAD), F32),
+            pltpu.VMEM((z, rows // z, width), BF16),
+            pltpu.VMEM((z, rows // z, width), BF16),
+            pltpu.VMEM((z, rows // z, width), BF16),
+            pltpu.VMEM((slots, n, BEAMS, HEAD), F32),
+            pltpu.VMEM((2, slots, n * GROUP * BEAMS, BLOCK), F32),
+            pltpu.VMEM((gk.shape[0] + 8, HEAD), F32),
+            pltpu.VMEM((gk.shape[0] + 8, HEAD), F32),
         ]
         + sems,
         compiler_params=pltpu.CompilerParams(
@@ -369,9 +394,17 @@
         name="decode_step",
     )(
         parents, lengths, bounds, table,
-        embeds, attn_norm.reshape(1, width), mlp_norm.reshape(1, width),
+        embeds, attn_norm, mlp_norm,
         wqkv, w_out, w_gate, w_up, w_down, pk, pv, gk, gv,
     )
+    return pl.pallas_call(
+        store,
+        out_shape=tuple(jax.ShapeDtypeStruct(a.shape, a.dtype) for a in results),
+        in_specs=[hbm] * 3,
+        out_specs=(hbm,) * 3,
+        scratch_shapes=[pltpu.SemaphoreType.DMA((3,))],
+        name="store_results",
+    )(*results)
 
 
 def solution(mesh):

time: 70.4 us -> 93.4 us (1.33)
  Pallas kernels: 58.8 us -> 92.6 us
  local copies, waits for them, and re-layouts: 10.7 us -> 0 us
    pallas_call x0 -> x1, Pallas kernels: none -> 35.9 us  [body(): pl.pallas_call(store, out_shape=tuple((jax.ShapeDtypeStruct(a.shape, a.dt...]
    unnamed x7 -> x0, local copies, waits for them, and re-layouts: 8.15 us -> none
    reshape x2 -> x0, local copies, waits for them, and re-layouts: 2.5 us -> none  [the longest x1 1.25 us: body(): mlp_norm.reshape(1, width)]
    pallas_call x1, Pallas kernels: 58.8 us -> 56.7 us  [body(): pl.pallas_call(functools.partial(kernel, n, z, hk, slots, width, units),...]
where the time goes in v2:
time: 93.4 us; the launch traced here: 93.2 us
  Pallas kernels  92.6 us (99%)
    pallas_call x1, Pallas kernels, body(): pl.pallas_call(functools.partial(kernel, n, z, hk, slots, width, units),...  56.7 us
    pallas_call x1, Pallas kernels, body(): pl.pallas_call(store, out_shape=tuple((jax.ShapeDtypeStruct(a.shape, a.dt...  35.9 us

profile of v2, /device:TPU:0, one launch (start us, length us, event | category | flops | bytes accessed | tf_op | source)
XLA Modules:
  0.0 93.2 jit_solution(10002000879642329708)
XLA Ops:
  0.6 56.7 %decode_step.1 = (f32[1,64,384]{2,1,0:T(8,128)}, bf16[8,2,128,128]{3,2,1,0:T(8,128)(2,1)}, bf16[8,2,128,128]{3,2,1,0:T(8,128)(2,1)}) custom-call(s32[1,8]{1,0:T(1,128)} %parents.1, s32[8]{0:T(128)} %lengths.1, s32[5]{0:T(128)} %bounds.1, s32[32]{0:T(128)} %table.1, bf16[1,64,384]{2,1,0:T(8,128)(2,1)} %embeds.1, f32[384]{0:T(512)} %attn_norm.1, f32[384]{0:T(512)} %mlp_norm.1, ...), custom_call_target="tpu_custom_call" | custom-call | tf_op jit(solution)/shard_map/decode_step/pallas_call | solution.py:362
  57.4 35.9 %store_results.1 = (f32[1,64,384]{2,1,0:T(8,128)}, bf16[8,2,128,128]{3,2,1,0:T(8,128)(2,1)}, bf16[8,2,128,128]{3,2,1,0:T(8,128)(2,1)}) custom-call(f32[1,64,384]{2,1,0:T(8,128)} %get-tuple-element.6.refs_0_, bf16[8,2,128,128]{3,2,1,0:T(8,128)(2,1)} %get-tuple-element.7.refs_1_, bf16[8,2,128,128]{3,2,1,0:T(8,128)(2,1)} %get-tuple-element.8.refs_2_), custom_call_target="tpu_custom_call" | custom-call | tf_op jit(solution)/shard_map/store_results/pallas_call | solution.py:400

commit v3 on v2

--- a/solution.py
+++ b/solution.py
@@ -45,9 +45,9 @@
     wqkv_h, wout_h, wgate_h, wup_h, wdown_h, pk_h, pv_h, gk_h, gv_h,
     hidden_out, keys_out, values_out,
     wqkv, wout, wgate, wup, wdown, pk, pv, gk, gv, local_sem,
-    qs, qr, qall, os_, orx, oall, ks, kr, ka, gs, gr, hall, fs, fr, fa,
+    qs, qr, qall, os_, orx, oall, kr, gs, gr, hall, fr, kc, vc,
     bias, sbuf, gkf, gvf,
-    s1, r1, s2, r2, s3, r3, s4, r4, s5, r5, s6, r6, s7, r7, s8, r8, s9, r9, s10, r10,
+    s1, r1, s2, r2, s3, r3, s4, r4, s5, r5, s6, r6, s7, r7, s8, r8,
 ):
     b = lax.axis_index("blk")
     k = lax.axis_index("kv")
@@ -55,6 +55,16 @@
     own_q = hk * GROUP * BEAMS
     per_head = GROUP * BEAMS
     scale = 1.0 / math.sqrt(HEAD)
+
+    barrier = pltpu.get_barrier_semaphore()
+
+    @pl.loop(1, n)
+    def _(d):
+        pl.semaphore_signal(barrier, inc=1, device_id={"blk": lax.rem(b + d, n)}, device_id_type=MESH)
+
+    @pl.loop(1, z)
+    def _(d):
+        pl.semaphore_signal(barrier, inc=1, device_id={"kv": lax.rem(k + d, z)}, device_id_type=MESH)
 
     loads = [
         pltpu.make_async_copy(src, dst, local_sem.at[i])
@@ -67,16 +77,6 @@
         load.start()
     l_qkv, l_gk, l_gv, l_pk, l_pv, l_out, l_gate, l_up, l_down = loads
 
-    barrier = pltpu.get_barrier_semaphore()
-
-    @pl.loop(1, n)
-    def _(d):
-        pl.semaphore_signal(barrier, inc=1, device_id={"blk": lax.rem(b + d, n)}, device_id_type=MESH)
-
-    @pl.loop(1, z)
-    def _(d):
-        pl.semaphore_signal(barrier, inc=1, device_id={"kv": lax.rem(k + d, z)}, device_id_type=MESH)
-
     def exchange(axis, me, size, src_of, dst, ssem, rsem):
         def copy(other, slot):
             return pltpu.make_async_remote_copy(
@@ -108,25 +108,19 @@
     x_q = blk(lambda t: qall.at[b], qall, s2, r2)
     x_o = blk(lambda t: os_.at[t], orx, s3, r3)
     x_heads = blk(lambda t: oall.at[b], oall, s4, r4)
-    x_attn = kvx(lambda t: ks.at[t], kr, s5, r5)
-    x_attn2 = kvx(lambda t: ka.at[k], ka, s9, r9)
+    x_attn = kvx(lambda t: kr.at[k], kr, s5, r5)
     x_mix = blk(lambda t: gs.at[t], gr, s6, r6)
     x_hid = blk(lambda t: hall.at[b], hall, s7, r7)
-    x_ff = kvx(lambda t: fs.at[t], fr, s8, r8)
-    x_ff2 = kvx(lambda t: fa.at[k], fa, s10, r10)
-
-    def over_kv(part, send, got, every, scatter, gather):
-        send[...] = part.reshape(send.shape).astype(BF16)
-        got[k] = send[k]
-        scatter[0]()
-        scatter[1]()
-        summed = got[0].astype(F32)
+    x_ff = kvx(lambda t: fr.at[k], fr, s8, r8)
+
+    def over_kv(part, every, exchanged):
+        every[k] = part.astype(BF16)
+        exchanged[0]()
+        exchanged[1]()
+        summed = every[0].astype(F32)
         for t in range(1, z):
-            summed = summed + got[t].astype(F32)
-        every[k] = summed.astype(BF16)
-        gather[0]()
-        gather[1]()
-        return every[...].astype(F32).reshape(rows, width)
+            summed = summed + every[t].astype(F32)
+        return summed
 
     residual = embeds[0].astype(F32)
     squares = jnp.sum(residual * residual, axis=1, keepdims=True)
@@ -142,15 +136,16 @@
         load.start()
     lane = lax.broadcasted_iota(jnp.int32, (BEAMS, HEAD), 1)
 
-    @pl.loop(0, n)
-    def _(t):
-        tenant = sum((t >= bounds[i]).astype(jnp.int32) for i in range(1, TENANTS))
-        last = lengths[t]
-
-        @pl.loop(0, slots)
-        def _(i):
-            place = table[i] * BLOCK - tenant * PROMPT + lane
-            bias[i, t] = jnp.where((place >= 0) & (place < last), 0.0, MASKED)
+    firsts = [
+        sum((t >= bounds[i]).astype(jnp.int32) for i in range(1, TENANTS)) * PROMPT for t in range(n)
+    ]
+
+    @pl.loop(0, slots)
+    def _(i):
+        start = table[i] * BLOCK
+        for t in range(n):
+            place = lane + (start - firsts[t])
+            bias[i, t] = jnp.where((place >= 0) & (place < lengths[t]), 0.0, MASKED)
 
     for load, src, dst in ((l_gk, gk, gkf), (l_gv, gv, gvf)):
         load.wait()
@@ -187,8 +182,8 @@
 
     row = lax.broadcasted_iota(jnp.int32, (BLOCK, HEAD), 0)
     new = [
-        ([rotated(piece(h, GROUP)) for h in range(hk)], gkf, keys_out),
-        ([piece(h, GROUP + 1) for h in range(hk)], gvf, values_out),
+        ([rotated(piece(h, GROUP)) for h in range(hk)], gkf, kc),
+        ([piece(h, GROUP + 1) for h in range(hk)], gvf, vc),
     ]
     for i in range(BEAMS):
         parent = parents[0, i]
@@ -198,12 +193,18 @@
                 old = src[pl.ds(first, BLOCK, stride=hk) if hk > 1 else pl.ds(first, BLOCK), :]
                 dst[i, h] = jnp.where(row == EARLIER, rows_new[h][i : i + 1], old).astype(BF16)
 
+    stores = [
+        pltpu.make_async_copy(kc, keys_out, local_sem.at[9]),
+        pltpu.make_async_copy(vc, values_out, local_sem.at[10]),
+    ]
+    for copy in stores:
+        copy.start()
     own_f = own_query.astype(F32)
     gen = []
     for h in range(hk):
         query = own_f[h * per_head : (h + 1) * per_head].astype(BF16)
-        keys = keys_out[:, h].reshape(BEAMS * BLOCK, HEAD)
-        vals = values_out[:, h].reshape(BEAMS * BLOCK, HEAD)
+        keys = kc[:, h].reshape(BEAMS * BLOCK, HEAD)
+        vals = vc[:, h].reshape(BEAMS * BLOCK, HEAD)
         scores = dot_t(query, keys) * scale
         beam = lax.broadcasted_iota(jnp.int32, scores.shape, 0) % BEAMS
         owner = lax.broadcasted_iota(jnp.int32, scores.shape, 1) // BLOCK
@@ -288,7 +289,7 @@
     ).astype(BF16)
     l_out.wait()
     after = residual + over_kv(
-        jnp.dot(heads, wout[...], preferred_element_type=F32), ks, kr, ka, x_attn, x_attn2
+        jnp.dot(heads, wout[...], preferred_element_type=F32), kr, x_attn
     )
 
     squares = jnp.sum(after * after, axis=1, keepdims=True)
@@ -323,10 +324,12 @@
     ).astype(BF16)
     l_down.wait()
     hidden_out[0] = after + over_kv(
-        jnp.dot(hidden, wdown[...], preferred_element_type=F32), fs, fr, fa, x_ff, x_ff2
+        jnp.dot(hidden, wdown[...], preferred_element_type=F32), fr, x_ff
     )
 
-    for x in (x_qkv, x_q, x_o, x_heads, x_attn, x_attn2, x_mix, x_hid, x_ff, x_ff2):
+    for copy in stores:
+        copy.wait()
+    for x in (x_qkv, x_q, x_o, x_heads, x_attn, x_mix, x_hid, x_ff):
         x[2]()
 
 
@@ -357,15 +360,15 @@
     cache = jax.ShapeDtypeStruct((BEAMS, hk, BLOCK, HEAD), BF16)
     wide = hk * COLS + HEAD
     sems = []
-    for size in (n, n, n, n, z, n, n, z, z, z):
+    for size in (n, n, n, n, z, n, n, z):
         sems += [pltpu.SemaphoreType.DMA((size,))] * 2
     results = pl.pallas_call(
         functools.partial(kernel, n, z, hk, slots, width, units),
         out_shape=(jax.ShapeDtypeStruct((1, rows, width), F32), cache, cache),
         in_specs=[smem] * 4 + [vmem] * 3 + [hbm] * 9,
-        out_specs=(vmem, vmem, vmem),
+        out_specs=(vmem, hbm, hbm),
         scratch_shapes=like
-        + [pltpu.SemaphoreType.DMA((9,))]
+        + [pltpu.SemaphoreType.DMA((11,))]
         + [
             pltpu.VMEM((n, BEAMS, wide), F32),
             pltpu.VMEM((n, BEAMS, wide), F32),
@@ -373,15 +376,13 @@
             pltpu.VMEM((n, own_q, 2 * HEAD), BF16),
             pltpu.VMEM((n, own_q, 2 * HEAD), BF16),
             pltpu.VMEM((n, own_q, HEAD), BF16),
-            pltpu.VMEM((z, rows // z, width), BF16),
-            pltpu.VMEM((z, rows // z, width), BF16),
-            pltpu.VMEM((z, rows // z, width), BF16),
+            pltpu.VMEM((z, rows, width), BF16),
             pltpu.VMEM((n, 2 * BEAMS, units + HEAD), BF16),
             pltpu.VMEM((n, 2 * BEAMS, units + HEAD), BF16),
             pltpu.VMEM((n, 2 * BEAMS, units // 2), BF16),
-            pltpu.VMEM((z, rows // z, width), BF16),
-            pltpu.VMEM((z, rows // z, width), BF16),
-            pltpu.VMEM((z, rows // z, width), BF16),
+            pltpu.VMEM((z, rows, width), BF16),
+            pltpu.VMEM(cache.shape, BF16),
+            pltpu.VMEM(cache.shape, BF16),
             pltpu.VMEM((slots, n, BEAMS, HEAD), F32),
             pltpu.VMEM((2, slots, n * GROUP * BEAMS, BLOCK), F32),
             pltpu.VMEM((gk.shape[0] + 8, HEAD), F32),
@@ -401,7 +402,7 @@
         store,
         out_shape=tuple(jax.ShapeDtypeStruct(a.shape, a.dtype) for a in results),
         in_specs=[hbm] * 3,
-        out_specs=(hbm,) * 3,
+        out_specs=(vmem,) * 3,
         scratch_shapes=[pltpu.SemaphoreType.DMA((3,))],
         name="store_results",
     )(*results)

time: 93.4 us -> 57.4 us (0.61)
  Pallas kernels: 92.6 us -> 56.6 us
    pallas_call x1, Pallas kernels: 35.9 us -> 2.28 us  [body(): pl.pallas_call(store, out_shape=tuple((jax.ShapeDtypeStruct(a.shape, a.dt...]
    pallas_call x1, Pallas kernels: 56.7 us -> 54.3 us  [body(): pl.pallas_call(functools.partial(kernel, n, z, hk, slots, width, units),...]
where the time goes in v3:
time: 57.4 us; the launch traced here: 57.2 us
  Pallas kernels  56.6 us (99%)
  between operations  0.65 us (1%)
    pallas_call x1, Pallas kernels, body(): pl.pallas_call(functools.partial(kernel, n, z, hk, slots, width, units),...  54.3 us
    pallas_call x1, Pallas kernels, body(): pl.pallas_call(store, out_shape=tuple((jax.ShapeDtypeStruct(a.shape, a.dt...  2.28 us

profile of v3, /device:TPU:0, one launch (start us, length us, event | category | flops | bytes accessed | tf_op | source)
XLA Modules:
  0.0 57.2 jit_solution(5257287363220564024)
XLA Ops:
  0.6 54.3 %decode_step.1 = (f32[1,64,384]{2,1,0:T(8,128)}, bf16[8,2,128,128]{3,2,1,0:T(8,128)(2,1)}, bf16[8,2,128,128]{3,2,1,0:T(8,128)(2,1)}) custom-call(s32[1,8]{1,0:T(1,128)} %parents.1, s32[8]{0:T(128)} %lengths.1, s32[5]{0:T(128)} %bounds.1, s32[32]{0:T(128)} %table.1, bf16[1,64,384]{2,1,0:T(8,128)(2,1)} %embeds.1, f32[384]{0:T(512)} %attn_norm.1, f32[384]{0:T(512)} %mlp_norm.1, ...), custom_call_target="tpu_custom_call" | custom-call | tf_op jit(solution)/shard_map/decode_step/pallas_call | solution.py:365
  54.9 2.3 %store_results.1 = (f32[1,64,384]{2,1,0:T(8,128)}, bf16[8,2,128,128]{3,2,1,0:T(8,128)(2,1)}, bf16[8,2,128,128]{3,2,1,0:T(8,128)(2,1)}) custom-call(f32[1,64,384]{2,1,0:T(8,128)} %get-tuple-element.6.refs_0_, bf16[8,2,128,128]{3,2,1,0:T(8,128)(2,1)} %get-tuple-element.7.refs_1_, bf16[8,2,128,128]{3,2,1,0:T(8,128)(2,1)} %get-tuple-element.8.refs_2_), custom_call_target="tpu_custom_call" | custom-call | tf_op jit(solution)/shard_map/store_results/pallas_call | solution.py:401

commit v4 on v3

--- a/solution.py
+++ b/solution.py
@@ -220,7 +220,7 @@
     l_pk.wait()
     l_pv.wait()
     all_rows = n * per_head
-    chunk = min(8, slots)
+    chunk = min(16, slots)
     queries = qall[...].astype(F32)
     heads_q = [
         queries[:, h * per_head : (h + 1) * per_head].reshape(all_rows, HEAD).astype(BF16)

time: 57.4 us -> 56.6 us (0.986)
  Pallas kernels: 56.6 us -> 55.7 us
    pallas_call x1, Pallas kernels: 54.3 us -> 53.5 us  [body(): pl.pallas_call(functools.partial(kernel, n, z, hk, slots, width, units),...]
where the time goes in v4:
time: 56.6 us; the launch traced here: 56.4 us
  Pallas kernels  55.7 us (98%)
  between operations  0.65 us (1%)
    pallas_call x1, Pallas kernels, body(): pl.pallas_call(functools.partial(kernel, n, z, hk, slots, width, units),...  53.5 us
    pallas_call x1, Pallas kernels, body(): pl.pallas_call(store, out_shape=tuple((jax.ShapeDtypeStruct(a.shape, a.dt...  2.28 us

profile of v4, /device:TPU:0, one launch (start us, length us, event | category | flops | bytes accessed | tf_op | source)
XLA Modules:
  0.0 56.4 jit_solution(7694049162582507009)
XLA Ops:
  0.6 53.5 %decode_step.1 = (f32[1,64,384]{2,1,0:T(8,128)}, bf16[8,2,128,128]{3,2,1,0:T(8,128)(2,1)}, bf16[8,2,128,128]{3,2,1,0:T(8,128)(2,1)}) custom-call(s32[1,8]{1,0:T(1,128)} %parents.1, s32[8]{0:T(128)} %lengths.1, s32[5]{0:T(128)} %bounds.1, s32[32]{0:T(128)} %table.1, bf16[1,64,384]{2,1,0:T(8,128)(2,1)} %embeds.1, f32[384]{0:T(512)} %attn_norm.1, f32[384]{0:T(512)} %mlp_norm.1, ...), custom_call_target="tpu_custom_call" | custom-call | tf_op jit(solution)/shard_map/decode_step/pallas_call | solution.py:365
  54.1 2.3 %store_results.1 = (f32[1,64,384]{2,1,0:T(8,128)}, bf16[8,2,128,128]{3,2,1,0:T(8,128)(2,1)}, bf16[8,2,128,128]{3,2,1,0:T(8,128)(2,1)}) custom-call(f32[1,64,384]{2,1,0:T(8,128)} %get-tuple-element.6.refs_0_, bf16[8,2,128,128]{3,2,1,0:T(8,128)(2,1)} %get-tuple-element.7.refs_1_, bf16[8,2,128,128]{3,2,1,0:T(8,128)(2,1)} %get-tuple-element.8.refs_2_), custom_call_target="tpu_custom_call" | custom-call | tf_op jit(solution)/shard_map/store_results/pallas_call | solution.py:401
